TPU v7x, 256 devices: a whole 4x4x8 slice. The times are simulated.
256 devices in a mesh: context: 16 (over z_lo, x), tensor: 16 (over z_hi, y, core).
Axes of the slice: x: 4, y: 4, z: 8 (z_hi: 2, z_lo: 4; z = z_hi * 4 + z_lo), core: 2. Of those that a mesh axis runs over, the one named last changes fastest.
Arguments:
- tokens: bfloat16 [32768, 4096], P(('context', 'tensor')), may hold values from -6 to 6
- norm_gain: bfloat16 [4096], replicated, may hold values from 0.5 to 1.5
- in_weight: bfloat16 [4096, 3, 4096], P(None, None, 'tensor'), may hold values from -0.09375 to 0.09375
- short_filter: bfloat16 [3, 3, 4096], P(None, None, 'tensor'), may hold values from -3.5 to 3.5
- long_filter: bfloat16 [256, 128], P('tensor'), may hold values from -0.5 to 0.5
- doc_start: int32 [32768], P('context'), may hold values from 0 to 32767, as said below
Outputs:
- layer_out: bfloat16 [32768, 4096], P(('context', 'tensor'))
Inputs may be any that keep to these rules, and one draw needn't show every extreme that they name: doc_start[0] = 0, and for t > 0 doc_start[t] is either doc_start[t - 1] or t, so documents are contiguous runs of positions; the last position begins a document.
All inputs are finite; a program needn't handle non-finite values.
Results may differ from a plain program's by a relative error of at most 0.0089.
Values may be sent and summed in bfloat16 or wider, within the bound.
No kernel may reach another device: no remote copies, remote signals or barrier semaphores. Data moves between devices by JAX's collectives and lax.ppermute only.
A program may use at most 128 MiB of HBM per device.

v0:
```python
import jax
import jax.numpy as jnp
from jax import lax
from jax.sharding import PartitionSpec as P


def from_behind(shard, axis, by):
    size = lax.axis_size(axis)
    pairs = [(i, i + by) for i in range(size) if 0 <= i + by < size]
    return lax.ppermute(shard, axis, pairs)


def banded(long_filter, span):
    groups = long_filter.shape[0]
    reversed_pad = jnp.concatenate(
        [long_filter[:, ::-1], jnp.zeros((groups, span), long_filter.dtype)], axis=1
    )
    tiled = jnp.tile(reversed_pad, (1, span))[:, : span * (2 * span - 1)]
    return tiled.reshape(groups, span, 2 * span - 1)


def short_mix(padded, positions, starts, filters):
    out_count = positions.shape[0]
    short_taps = filters.shape[1]
    summed = jnp.zeros((out_count,) + padded.shape[1:], jnp.float32)
    for lag_step in range(short_taps):
        begin = short_taps - 1 - lag_step
        rows_in = lax.slice_in_dim(padded, begin, begin + out_count, axis=0).astype(jnp.float32)
        kept_mask = (positions - lag_step >= starts)[:, None, None]
        summed = summed + jnp.where(
            kept_mask, filters[:, lag_step, :].astype(jnp.float32)[None] * rows_in, 0.0
        )
    return summed


def per_device(tokens, norm_gain, in_weight, short_filter, long_filter, doc_start):
    width = tokens.shape[1]
    channels = in_weight.shape[2]
    groups = long_filter.shape[0]
    span = long_filter.shape[1]
    share = channels // groups
    short_taps = short_filter.shape[1]
    float_tokens = tokens.astype(jnp.float32)
    scale_rows = lax.rsqrt(jnp.mean(float_tokens * float_tokens, axis=-1, keepdims=True) + 1e-06)
    normed = (float_tokens * scale_rows * norm_gain.astype(jnp.float32)[None]).astype(jnp.bfloat16)
    flat_weight = in_weight.reshape(width, 3 * channels)
    projected = jnp.dot(
        lax.all_gather(normed, "tensor", axis=0, tiled=True),
        flat_weight,
        preferred_element_type=jnp.float32,
    ).astype(jnp.bfloat16)
    length = projected.shape[0]
    projected = projected.reshape(length, 3, channels)
    starts = doc_start - lax.axis_index("context") * length
    local_rows = jnp.arange(length, dtype=jnp.int32)
    rim_rows = from_behind(projected[length - (short_taps - 1) :], "context", 1)
    padded = jnp.concatenate([rim_rows, projected], axis=0)
    mixed = short_mix(padded, local_rows, starts, short_filter)
    key_value = (mixed[:, 1] * mixed[:, 2]).astype(jnp.bfloat16)
    tail_rows = from_behind(key_value[length - (span - 1) :], "context", 1)
    query = mixed[:, 0]
    extended = jnp.concatenate([tail_rows, key_value], axis=0)
    blocks = length // span
    head_part = extended[:length].reshape(blocks, span, channels)
    rest_part = jnp.concatenate([extended[span:], jnp.zeros((1, channels), jnp.bfloat16)], axis=0)
    rest_part = rest_part.reshape(blocks, span, channels)[:, : span - 1]
    window = jnp.concatenate([head_part, rest_part], axis=1).reshape(
        blocks, 2 * span - 1, groups, share
    )
    inputs = (
        (jnp.arange(blocks, dtype=jnp.int32) * span)[:, None]
        + jnp.arange(2 * span - 1, dtype=jnp.int32)[None]
        - (span - 1)
    )
    block_starts = starts.reshape(blocks, span)
    kept_mask = inputs[:, None, :] >= block_starts[:, :, None]
    toeplitz = banded(long_filter, span)
    weights = jnp.where(kept_mask[:, None], toeplitz[None], jnp.zeros((), jnp.bfloat16))
    conv = jnp.einsum(
        "bgij,bjgc->bigc", weights, window, preferred_element_type=jnp.float32
    ).reshape(length, channels)
    gated = (query * conv).astype(jnp.bfloat16)
    returned = lax.all_to_all(gated, "tensor", split_axis=0, concat_axis=1, tiled=True)
    return (float_tokens + returned.astype(jnp.float32)).astype(jnp.bfloat16)


def solution(mesh):
    in_specs = (
        P(("context", "tensor"), None),
        P(),
        P(None, None, "tensor"),
        P(None, None, "tensor"),
        P("tensor", None),
        P("context"),
    )
    out_specs = P(("context", "tensor"), None)
    return jax.shard_map(
        per_device, mesh=mesh, in_specs=in_specs, out_specs=out_specs, check_vma=False
    )
```

profile of v0, /device:TPU:70, one launch (start us, length us, event | category | flops | bytes accessed | tf_op | source)
XLA Modules:
  0.0 295.7 jit_solution(7310383108310972181)
XLA Ops:
  7.2 1.5 fusion.6
  8.8 2.5 fusion.8
  11.3 8.8 %copy.11 = bf16[4096,3,256]{0,2,1:T(8,128)(2,1)} copy(bf16[4096,3,256]{2,0,1:T(8,128)(2,1)} %param.8) | data formatting | bytes 12582912 | tf_op args[2]
  21.4 163.9 %all-gather.2.cloned.1.call-done = bf16[2048,4096]{1,0:T(8,128)(2,1)} async-done(((bf16[128,4096]{1,0:T(8,128)(2,1)}), bf16[2048,4096]{1,0:T(8,128)(2,1)}) %all-gather.2.cloned.1.call-update) | async-done | bytes 16777232 | tf_op jit(solution)/shard_map/all_gather | solution.py:48
  185.3 18.2 %convolution_convert_fusion = bf16[2048,768]{1,0:T(8,128)(2,1)S(1)} fusion(bf16[2048,4096]{1,0:T(8,128)(2,1)} %all-gather.2.cloned.1.call-done, bf16[4096,768]{0,1:T(8,128)(2,1)} %bitcast.46), kind=kOutput, calls=%fused_computation.6 | convolution fusion | flops 12886474752 | bytes 26214400 | tf_op jit(solution)/shard_map/dot_general | solution.py:47
  203.5 1.6 copy-done.1
  205.3 1.9 collective-permute-start
  208.4 3.2 %copy.12 = bf16[2048,768]{0,1:T(8,128)(2,1)S(1)} copy(bf16[2048,768]{1,0:T(8,128)(2,1)} %copy-done.1) | data formatting | bytes 6291456 | tf_op jit(solution)/shard_map/convert_element_type | solution.py:51
  211.6 2.6 collective-permute-done
  214.2 5.0 %select_add_fusion = f32[2048,3,256]{0,2,1:T(8,128)S(1)} fusion(bf16[2048,3,256]{0,2,1:T(8,128)(2,1)S(1)} %bitcast.43, bf16[2,3,256]{0,2,1:T(8,128)(2,1)S(1)} %collective-permute-done, f32[3,256]{1,0:T(4,128)} %get-tuple-element.13, f32[3,256]{1,0:T(4,128)} %get-tuple-element.14, f32[3,256]{1,0:T(4,128)} %bitcast.56, pred[2048]{0:T(1024)(128)(4,1)} %get-tuple-element.9, ...), kind=kLoop, calls=%fused_computation.5 | loop fusion | flops 26738688 | bytes 9455616 | tf_op jit(solution)/shard_map/add | solution.py:30
  219.3 1.9 slice_bitcast_fusion
  221.2 4.5 %collective-permute-start.1 = (bf16[127,256]{0,1:T(8,128)(2,1)S(1)}, bf16[127,256]{0,1:T(8,128)(2,1)S(1)}, u32[]{:S(2)}, u32[]{:S(2)}) collective-permute-start(bf16[127,256]{0,1:T(8,128)(2,1)S(1)} %slice_bitcast_fusion.1), channel_id=1, source_target_pairs={{0,16},{16,32},{32,48},{48,64},{64,80},{80,96},{96,112},{112,128},... | collective-permute-start | bytes 195080 | tf_op jit(solution)/shard_map/ppermute | solution.py:10
  225.7 1.2 broadcast_compare_fusion
  227.7 4.3 %broadcast_in_dim.65 = bf16[16,128,255]{2,1,0:T(8,128)(2,1)} reshape(bf16[16,32640]{1,0:T(8,128)(2,1)S(1)} %slice.77) | data formatting | bytes 2088960 | tf_op jit(solution)/shard_map/jit(_where)/broadcast_in_dim | solution.py:78
  233.6 1.4 copy.27
  235.0 2.0 copy.28
  237.1 1.2 pad_maximum_fusion.1
  238.3 1.5 copy.16
  240.4 0.7 copy-done.2
  241.1 5.8 %fusion = f32[16,16,16,128]{3,2,1,0:T(8,128)S(1)} fusion(pred[16,128,255]{2,1,0:T(8,128)(4,1)} %broadcast_compare_fusion, bf16[16,128,255]{2,1,0:T(8,128)(2,1)S(1)} %copy-done.2, bf16[16,127,16,16]{1,3,2,0:T(8,128)(2,1)} %bitcast.54, bf16[16,128,16,16]{1,3,2,0:T(8,128)(2,1)S(1)} %copy.19), kind=kOutput, calls=%fused_computation | convolution fusion | flops 279920640 | bytes 5752832 | tf_op jit(solution)/shard_map/bgij,bjgc->bigc/dot_general | solution.py:79
  246.9 0.7 fusion.14
  247.6 36.4 %all_to_all.10 = bf16[16,128,256]{1,2,0:T(8,128)(2,1)S(1)} all-to-all(bf16[16,128,256]{1,2,0:T(8,128)(2,1)S(1)} %fusion.14), channel_id=1, replica_groups=mesh['context'=16,'tensor'=16] {'tensor'}, dimensions={0} | all-to-all | bytes 2097152 | tf_op jit(solution)/shard_map/all_to_all | solution.py:83
  284.2 1.8 copy.23
  286.0 2.8 fusion.9
  (40 shorter events, 6.7 us)
Async XLA Ops:
  6.5 178.7 %all-gather.2.cloned.1.call-start = ((), (), s32[]{:S(2)}) async-start(), calls=%async_computation.1 | async-start | bytes 17825792 | tf_op jit(solution)/shard_map/all_gather | solution.py:48
  11.3 8.8 %copy-start.5 = (bf16[3,3,256]{2,1,0:T(4,128)(2,1)S(1)}, bf16[3,3,256]{2,1,0:T(4,128)(2,1)}, u32[]{:S(2)}) copy-start(bf16[3,3,256]{2,1,0:T(4,128)(2,1)} %param.9) | copy-start | bytes 13828
  11.3 9.4 %copy-start.4 = (s32[2048]{0:T(1024)S(1)}, s32[2048]{0:T(1024)}, u32[]{:S(2)}) copy-start(s32[2048]{0:T(1024)} %param.11) | copy-start | bytes 24580
  203.5 1.6 copy-start.1
  205.3 9.0 %collective-permute-start = (bf16[2,3,256]{0,2,1:T(8,128)(2,1)S(1)}, bf16[2,3,256]{0,2,1:T(8,128)(2,1)S(1)}, u32[]{:S(2)}, u32[]{:S(2)}) collective-permute-start(bf16[2,3,256]{0,2,1:T(8,128)(2,1)S(1)} %bitcast.55), channel_id=1, source_target_pairs={{0,16},{16,32},{32,48},{48,64},{64,80},{80,96},{96,112},{112,128},... | collective-permute-start | bytes 9224 | tf_op jit(solution)/shard_map/ppermute | solution.py:10
  219.2 6.5 %copy-start.3 = (s32[16,128]{1,0:T(8,128)S(1)}, s32[16,128]{1,0:T(8,128)}, u32[]{:S(2)}) copy-start(s32[16,128]{1,0:T(8,128)} %subtract_bitcast_fusion) | copy-start | bytes 24580
  219.2 7.6 %copy-start.6 = (bf16[16,128]{1,0:T(8,128)(2,1)S(1)}, bf16[16,128]{1,0:T(8,128)(2,1)}, u32[]{:S(2)}) copy-start(bf16[16,128]{1,0:T(8,128)(2,1)} %param.10) | copy-start | bytes 12292
  221.2 15.8 %collective-permute-start.1 = (bf16[127,256]{0,1:T(8,128)(2,1)S(1)}, bf16[127,256]{0,1:T(8,128)(2,1)S(1)}, u32[]{:S(2)}, u32[]{:S(2)}) collective-permute-start(bf16[127,256]{0,1:T(8,128)(2,1)S(1)} %slice_bitcast_fusion.1), channel_id=1, source_target_pairs={{0,16},{16,32},{32,48},{48,64},{64,80},{80,96},{96,112},{112,128},... | collective-permute-start | bytes 195080 | tf_op jit(solution)/shard_map/ppermute | solution.py:10
  239.8 1.2 copy-start.2
  284.0 2.0 copy-start
Sparse Core Ops, SparseCore 0:
  11.4 173.7 all-gather.1
where the time goes:
time: 296 us
  waiting for transfers between devices  167 us (56%)
  blocking collectives  36.4 us (12%)
  local copies, waits for them, and re-layouts  29.7 us (10%)
  matrix products  24 us (8%)
  other arithmetic  19 us (6%)
  between operations  13.6 us (5%)
  starting transfers between devices  6.41 us (2%)
    all_gather x1, waiting for transfers between devices, per_device(): lax.all_gather(normed, 'tensor', axis=0, tiled=True)  164 us
    all_to_all x1, blocking collectives, per_device(): lax.all_to_all(gated, 'tensor', split_axis=0, concat_axis=1, tiled=True)  36.4 us
    dot_general x1, matrix products, per_device(): jnp.dot(lax.all_gather(normed, 'tensor', axis=0, tiled=True), flat_weight...  18.2 us
    unnamed x21, local copies, waits for them, and re-layouts  16.5 us
    ppermute x2, starting transfers between devices, from_behind(): return lax.ppermute(shard, axis, pairs)  6.41 us
  transfers between devices with their start and end apart: 3, of which 2 were waited for; matrix products, arithmetic and copies ran while one was open for 9% of the time, Pallas kernels for 0%

commit v1 on v0

--- a/solution.py
+++ b/solution.py
@@ -80,7 +80,12 @@
         "bgij,bjgc->bigc", weights, window, preferred_element_type=jnp.float32
     ).reshape(length, channels)
     gated = (query * conv).astype(jnp.bfloat16)
-    returned = lax.all_to_all(gated, "tensor", split_axis=0, concat_axis=1, tiled=True)
+    returned = jnp.concatenate(
+        lax.all_to_all(
+            jnp.stack(jnp.split(gated, lax.axis_size("tensor"), axis=0)), "tensor", 0, 0
+        ),
+        axis=1,
+    )
     return (float_tokens + returned.astype(jnp.float32)).astype(jnp.bfloat16)
 
 

time: 296 us -> 297 us (level)
    unnamed x21 -> x37, local copies, waits for them, and re-layouts: 16.5 us -> 16 us
  transfers between devices with their start and end apart: 3 -> 3, of which waited for: 2 -> 2; matrix products, arithmetic and copies ran while one was open for 9% -> 8% of each run, Pallas kernels for 0% -> 0%
where the time goes in v1:
time: 297 us; the launch traced here: 296 us
  waiting for transfers between devices  167 us (56%)
  blocking collectives  36.4 us (12%)
  local copies, waits for them, and re-layouts  30.5 us (10%)
  matrix products  24.7 us (8%)
  other arithmetic  17.9 us (6%)
  between operations  13.6 us (5%)
  starting transfers between devices  6.41 us (2%)
    all_gather x1, waiting for transfers between devices, per_device(): lax.all_gather(normed, 'tensor', axis=0, tiled=True)  164 us
    all_to_all x1, blocking collectives, per_device(): lax.all_to_all(jnp.stack(jnp.split(gated, lax.axis_size('tensor'), axis=0...  36.4 us
    dot_general x1, matrix products, per_device(): jnp.dot(lax.all_gather(normed, 'tensor', axis=0, tiled=True), flat_weight...  19.2 us
    unnamed x37, local copies, waits for them, and re-layouts  16 us
    ppermute x2, starting transfers between devices, from_behind(): return lax.ppermute(shard, axis, pairs)  6.41 us
  transfers between devices with their start and end apart: 3, of which 2 were waited for; matrix products, arithmetic and copies ran while one was open for 8% of the time, Pallas kernels for 0%

profile of v1, /device:TPU:70, one launch (start us, length us, event | category | flops | bytes accessed | tf_op | source)
XLA Modules:
  0.0 296.1 jit_solution(6178761900978824967)
XLA Ops:
  6.5 0.7 convert_element_type.75
  7.2 1.5 fusion.6
  8.8 2.5 fusion.8
  11.3 8.8 %copy.10 = bf16[4096,3,256]{0,2,1:T(8,128)(2,1)} copy(bf16[4096,3,256]{2,0,1:T(8,128)(2,1)} %param.8) | data formatting | bytes 12582912 | tf_op args[2]
  21.4 163.9 %all-gather.2.cloned.1.call-done = bf16[2048,4096]{1,0:T(8,128)(2,1)} async-done(((bf16[128,4096]{1,0:T(8,128)(2,1)}), bf16[2048,4096]{1,0:T(8,128)(2,1)}) %all-gather.2.cloned.1.call-update) | async-done | bytes 16777232 | tf_op jit(solution)/shard_map/all_gather | solution.py:48
  185.3 19.2 %convolution_convert_fusion = bf16[2048,768]{1,0:T(8,128)(2,1)} fusion(bf16[2048,4096]{1,0:T(8,128)(2,1)} %all-gather.2.cloned.1.call-done, bf16[4096,768]{0,1:T(8,128)(2,1)} %bitcast.112), kind=kOutput, calls=%fused_computation.6 | convolution fusion | flops 12886474752 | bytes 26214400 | tf_op jit(solution)/shard_map/dot_general | solution.py:47
  204.5 0.7 slice.68
  205.4 1.9 collective-permute-start
  208.5 3.2 %copy.11 = bf16[2048,768]{0,1:T(8,128)(2,1)S(1)} copy(bf16[2048,768]{1,0:T(8,128)(2,1)} %convolution_convert_fusion) | data formatting | bytes 6291456 | tf_op jit(solution)/shard_map/convert_element_type | solution.py:51
  211.7 2.7 collective-permute-done
  214.4 5.0 %select_add_fusion = f32[2048,3,256]{0,2,1:T(8,128)S(1)} fusion(bf16[2048,3,256]{0,2,1:T(8,128)(2,1)S(1)} %bitcast.109, bf16[2,3,256]{0,2,1:T(8,128)(2,1)S(1)} %collective-permute-done, f32[3,256]{1,0:T(4,128)} %get-tuple-element.11, f32[3,256]{1,0:T(4,128)} %get-tuple-element.12, f32[3,256]{1,0:T(4,128)} %bitcast.122, pred[2048]{0:T(1024)(128)(4,1)} %get-tuple-element.7, ...), kind=kLoop, calls=%fused_computation.5 | loop fusion | flops 26738688 | bytes 9455616 | tf_op jit(solution)/shard_map/add | solution.py:30
  219.4 2.6 copy-done
  222.4 4.5 %collective-permute-start.1 = (bf16[127,256]{0,1:T(8,128)(2,1)S(1)}, bf16[127,256]{0,1:T(8,128)(2,1)S(1)}, u32[]{:S(2)}, u32[]{:S(2)}) collective-permute-start(bf16[127,256]{0,1:T(8,128)(2,1)S(1)} %slice_bitcast_fusion.17), channel_id=1, source_target_pairs={{0,16},{16,32},{32,48},{48,64},{64,80},{80,96},{96,112},{112,128},... | collective-permute-start | bytes 195080 | tf_op jit(solution)/shard_map/ppermute | solution.py:10
  226.9 1.1 broadcast_compare_fusion
  228.9 4.3 %broadcast_in_dim.65 = bf16[16,128,255]{2,1,0:T(8,128)(2,1)} reshape(bf16[16,32640]{1,0:T(8,128)(2,1)S(1)} %slice.77) | data formatting | bytes 2088960 | tf_op jit(solution)/shard_map/jit(_where)/broadcast_in_dim | solution.py:78
  234.8 1.4 copy.25
  236.5 0.6 copy.15
  237.7 0.7 copy-done.3
  238.5 5.5 %fusion.15 = f32[16,128,16,16]{1,3,2,0:T(8,128)S(1)} fusion(pred[16,128,255]{2,1,0:T(8,128)(4,1)} %broadcast_compare_fusion, bf16[16,128,255]{2,1,0:T(8,128)(2,1)S(1)} %copy-done.2, bf16[16,127,16,16]{1,3,2,0:T(8,128)(2,1)S(1)} %bitcast.120, bf16[16,128,16,16]{1,3,2,0:T(8,128)(2,1)S(1)} %copy.18), kind=kOutput, calls=%fused_computation.26 | convolution fusion | flops 279920640 | bytes 5752832 | tf_op jit(solution)/shard_map/bgij,bjgc->bigc/dot_general | solution.py:79
  243.9 1.2 copy.19
  245.2 2.3 fusion.10
  248.0 36.4 %all_to_all.5 = bf16[16,128,256]{1,2,0:T(8,128)(2,1)S(1)} all-to-all(bf16[16,128,256]{1,2,0:T(8,128)(2,1)S(1)} %fusion.20), channel_id=1, replica_groups=mesh['context'=16,'tensor'=16] {'tensor'}, dimensions={0} | all-to-all | bytes 2097152 | tf_op jit(solution)/shard_map/all_to_all | solution.py:84
  284.6 1.8 copy.20
  286.5 2.8 fusion.9
  (58 shorter events, 7.0 us)
Async XLA Ops:
  6.5 178.7 %all-gather.2.cloned.1.call-start = ((), (), s32[]{:S(2)}) async-start(), calls=%async_computation.1 | async-start | bytes 17825792 | tf_op jit(solution)/shard_map/all_gather | solution.py:48
  11.3 8.8 %copy-start.6 = (bf16[3,3,256]{2,1,0:T(4,128)(2,1)S(1)}, bf16[3,3,256]{2,1,0:T(4,128)(2,1)}, u32[]{:S(2)}) copy-start(bf16[3,3,256]{2,1,0:T(4,128)(2,1)} %param.9) | copy-start | bytes 13828
  11.3 9.4 %copy-start.5 = (s32[2048]{0:T(1024)S(1)}, s32[2048]{0:T(1024)}, u32[]{:S(2)}) copy-start(s32[2048]{0:T(1024)} %param.11) | copy-start | bytes 24580
  205.4 9.0 %collective-permute-start = (bf16[2,3,256]{0,2,1:T(8,128)(2,1)S(1)}, bf16[2,3,256]{0,2,1:T(8,128)(2,1)S(1)}, u32[]{:S(2)}, u32[]{:S(2)}) collective-permute-start(bf16[2,3,256]{0,2,1:T(8,128)(2,1)S(1)} %bitcast.121), channel_id=1, source_target_pairs={{0,16},{16,32},{32,48},{48,64},{64,80},{80,96},{96,112},{112,128},... | collective-permute-start | bytes 9224 | tf_op jit(solution)/shard_map/ppermute | solution.py:10
  219.4 2.6 copy-start
  222.0 4.9 %copy-start.4 = (s32[16,128]{1,0:T(8,128)S(1)}, s32[16,128]{1,0:T(8,128)}, u32[]{:S(2)}) copy-start(s32[16,128]{1,0:T(8,128)} %subtract_bitcast_fusion) | copy-start | bytes 24580
  222.0 6.0 %copy-start.7 = (bf16[16,128]{1,0:T(8,128)(2,1)S(1)}, bf16[16,128]{1,0:T(8,128)(2,1)}, u32[]{:S(2)}) copy-start(bf16[16,128]{1,0:T(8,128)(2,1)} %param.10) | copy-start | bytes 12292
  222.4 13.8 %collective-permute-start.1 = (bf16[127,256]{0,1:T(8,128)(2,1)S(1)}, bf16[127,256]{0,1:T(8,128)(2,1)S(1)}, u32[]{:S(2)}, u32[]{:S(2)}) collective-permute-start(bf16[127,256]{0,1:T(8,128)(2,1)S(1)} %slice_bitcast_fusion.17), channel_id=1, source_target_pairs={{0,16},{16,32},{32,48},{48,64},{64,80},{80,96},{96,112},{112,128},... | collective-permute-start | bytes 195080 | tf_op jit(solution)/shard_map/ppermute | solution.py:10
  236.5 1.2 copy-start.2
  237.2 1.3 copy-start.3
  284.4 2.0 copy-start.1
Sparse Core Ops, SparseCore 0:
  11.4 173.7 all-gather.1
